TPU v7x, 32 devices: a whole 2x2x4 slice. The times are simulated.
32 devices in a mesh: comp: 4 (over z), space: 8 (over y, x, core).
Axes of the slice: x: 2, y: 2, z: 4, core: 2. Of those that a mesh axis runs over, the one named last changes fastest.
Arguments:
- spectrum: float32 [36, 32, 64, 512], P('comp', None, 'space'), may hold values from 0.1 to 2
- sea_mask: int32 [64, 512], P('space'), may hold values from 0 to 1, as said below
- depth_class: int32 [64, 512], P('space'), may hold values from 0 to 3
- speed_table: float32 [4, 32], replicated, may hold values from 0.1 to 0.45
- depth_slope: float32 [2, 64, 512], P(None, 'space'), may hold values from -1 to 1
- turn_gain: float32 [32], replicated, may hold values from 0.05 to 0.3
- wind_vector: float32 [2, 64, 512], P(None, 'space'), may hold values from -4 to 4
Outputs:
- spectrum_out: float32 [36, 32, 64, 512], P('comp', None, 'space')
Inputs may be any that keep to these rules, and one draw needn't show every extreme that they name: `sea_mask`: 1 marks sea and 0 land; the land share of a row grows from about 5 percent in row 0 to about 75 percent in row 63.
All inputs are finite; a program needn't handle non-finite values.
Results may differ from a plain program's by a relative error of at most 0.0003.
Values sent between devices are 32-bit elements; how exact they have to be, the bound alone decides.
A program may use at most 192 MiB of HBM per device.

v0:
```python
import math

import jax
import jax.numpy as jnp
from jax import lax
from jax.sharding import PartitionSpec as P


def with_halo(block, sides, width, periodic):
    for axis, dim in sides:
        count = lax.axis_size(axis)
        forward = [(i, i + 1) for i in range(count - 1)]
        if periodic:
            forward.append((count - 1, 0))
        backward = [(target, source) for source, target in forward]
        low = lax.ppermute(
            lax.slice_in_dim(block, block.shape[dim] - width, None, axis=dim), axis, forward
        )
        high = lax.ppermute(lax.slice_in_dim(block, 0, width, axis=dim), axis, backward)
        block = jnp.concatenate([low, block, high], axis=dim)
    return block


def freq_ratio(frequencies):
    position = jnp.arange(frequencies).astype(jnp.float32)
    return jnp.exp((position - 0.5 * (frequencies - 1)) * math.log(1.1))


def masked_speeds(depth_class, speed_table, wet_mask):
    speeds = jnp.zeros((speed_table.shape[1],) + depth_class.shape, jnp.float32)
    for depth_level in range(speed_table.shape[0]):
        chosen = jnp.where(depth_class == depth_level, 1.0, 0.0).astype(jnp.float32)
        speeds = speeds + chosen[None] * speed_table[depth_level][:, None, None]
    return speeds * wet_mask


def quick_flux(behind, centre, forward, beyond, courant):
    magnitude = jnp.abs(courant)
    shape_term = (1.0 - magnitude * magnitude) / 6.0
    rightward = (
        0.5 * (centre + forward)
        - 0.5 * magnitude * (forward - centre)
        - shape_term * (forward - 2.0 * centre + behind)
    )
    leftward = (
        0.5 * (centre + forward)
        - 0.5 * magnitude * (centre - forward)
        - shape_term * (centre - 2.0 * forward + beyond)
    )
    return courant * jnp.where(courant >= 0.0, rightward, leftward)


def advect(padded, speeds, cosine, sine_dir):
    inside = padded.shape[-2] - 4
    centre = padded[..., 2 : inside + 2, :]
    middle = speeds[..., 2 : inside + 2, :]
    face_along = jnp.minimum(middle, jnp.roll(middle, -1, -1)) * cosine
    flux_along = quick_flux(
        jnp.roll(centre, 1, -1),
        centre,
        jnp.roll(centre, -1, -1),
        jnp.roll(centre, -2, -1),
        face_along,
    )
    face_across = (
        jnp.minimum(speeds[..., 1 : inside + 2, :], speeds[..., 2 : inside + 3, :]) * sine_dir
    )
    flux_across = quick_flux(
        padded[..., 0 : inside + 1, :],
        padded[..., 1 : inside + 2, :],
        padded[..., 2 : inside + 3, :],
        padded[..., 3 : inside + 4, :],
        face_across,
    )
    return (
        centre
        - (flux_along - jnp.roll(flux_along, 1, -1))
        - (flux_across[..., 1:, :] - flux_across[..., :-1, :])
    )


def refract(extended, turning):
    inside = extended.shape[0] - 4
    face_turn = 0.5 * (turning[1 : inside + 2] + turning[2 : inside + 3])
    flux_turn = quick_flux(
        extended[0 : inside + 1],
        extended[1 : inside + 2],
        extended[2 : inside + 3],
        extended[3 : inside + 4],
        face_turn,
    )
    return extended[2 : inside + 2] - (flux_turn[1:] - flux_turn[:-1])


def apply_sources(waves, energy, moment, wind_vector, wet_mask, cosine, sine_dir, freq_scale):
    mean_freq = moment / jnp.maximum(energy, 0.25)
    steepness = energy * mean_freq * mean_freq / 4.0
    projected = wind_vector[0] * cosine + wind_vector[1] * sine_dir
    growth = 0.2 * jnp.maximum(projected * freq_scale - 1.0, 0.0)
    damping = 0.25 * freq_scale * freq_scale * (steepness * steepness / jnp.maximum(mean_freq, 0.5))
    return waves * (1.0 + growth) / (1.0 + damping) * wet_mask


def local(spectrum, sea_mask, depth_class, speed_table, depth_slope, turn_gain, wind_vector):
    directions, frequencies, row_count, columns = spectrum.shape
    groups = lax.axis_size("comp")
    all_dirs = directions * groups
    offset = lax.axis_index("comp") * directions
    wet_mask = sea_mask.astype(jnp.float32)
    speeds = masked_speeds(depth_class, speed_table, wet_mask)
    step_angle = 2.0 * math.pi / all_dirs
    angles = ((offset + jnp.arange(directions)).astype(jnp.float32) + 0.5) * step_angle
    cosine = jnp.cos(angles)[:, None, None, None]
    sine_dir = jnp.sin(angles)[:, None, None, None]
    ext_index = (offset - 2 + jnp.arange(directions + 4)).astype(jnp.float32)
    ext_angles = (ext_index + 0.5) * step_angle
    ext_sine = jnp.sin(ext_angles)[:, None, None, None]
    ext_cosine = jnp.cos(ext_angles)[:, None, None, None]
    speed_ext = with_halo(speeds, (("space", 1),), 4, False)
    waves = spectrum * wet_mask
    for substep in range(2):
        padded = with_halo(waves, (("space", 2),), 2, False)
        waves = advect(padded, speed_ext[:, 2:-2, :], cosine, sine_dir)
    turning = (
        turn_gain[None, :, None, None]
        * (ext_sine * depth_slope[0] - ext_cosine * depth_slope[1])
        * wet_mask
    )
    extended = with_halo(waves, (("comp", 0),), 2, True)
    waves = refract(extended, turning)
    ratios = freq_ratio(frequencies)
    weights = ratios / (all_dirs * jnp.sum(ratios))
    freq_scale = ratios[None, :, None, None]
    weighted = waves * weights[None, :, None, None]
    energy, moment = lax.psum(
        (jnp.sum(weighted, axis=(0, 1)), jnp.sum(weighted * freq_scale, axis=(0, 1))), "comp"
    )
    return apply_sources(waves, energy, moment, wind_vector, wet_mask, cosine, sine_dir, freq_scale)


def solution(mesh):
    in_specs = (
        P("comp", None, "space", None),
        P("space", None),
        P("space", None),
        P(),
        P(None, "space", None),
        P(),
        P(None, "space", None),
    )
    out_specs = P("comp", None, "space", None)
    return jax.shard_map(local, mesh=mesh, in_specs=in_specs, out_specs=out_specs, check_vma=False)
```

profile of v0, /device:TPU:2, one launch (start us, length us, event | category | flops | bytes accessed | tf_op | source)
XLA Modules:
  0.0 200.7 jit_solution(15582560805376680759)
XLA Ops:
  0.0 0.7 convert_element_type.41
  0.7 0.7 compare_select_fusion.3
  1.4 0.8 slice_bitcast_fusion.7
  2.3 0.2 add_multiply_fusion
  2.5 1.0 fusion.83
  3.5 1.9 collective-permute-start
  5.4 3.6 %collective-permute-start.1 = (f32[32,4,512]{2,0,1:T(8,128)}, f32[32,4,512]{2,0,1:T(8,128)}, u32[]{:S(2)}, u32[]{:S(2)}) collective-permute-start(f32[32,4,512]{2,0,1:T(8,128)} %get-tuple-element.25), channel_id=1, source_target_pairs={{1,0},{2,1},{3,2},{4,3},{5,4},{6,5},{7,6},{9,8},{10,9},{11,10},{12... | collective-permute-start | bytes 786440 | tf_op jit(solution)/shard_map/ppermute | solution.py:19
  9.0 5.1 %copy_multiply_fusion = f32[9,32,8,512]{3,1,2,0:T(8,128)S(1)} fusion(f32[9,32,8,512]{3,2,1,0:T(8,128)} %param.7, f32[8,512]{1,0:T(8,128)S(1)} %convert_element_type.41), kind=kLoop, calls=%fused_computation.107 | loop fusion | flops 1179648 | bytes 9453568 | tf_op jit(solution)/shard_map/mul | solution.py:120
  14.2 0.0 copy-start
  14.2 1.8 fusion.82
  15.9 1.9 collective-permute-start.2
  17.9 3.6 %collective-permute-start.3 = (f32[9,32,2,512]{3,1,2,0:T(8,128)}, f32[9,32,2,512]{3,1,2,0:T(8,128)}, u32[]{:S(2)}, u32[]{:S(2)}) collective-permute-start(f32[9,32,2,512]{3,1,2,0:T(8,128)} %get-tuple-element.23), channel_id=1, source_target_pairs={{1,0},{2,1},{3,2},{4,3},{5,4},{6,5},{7,6},{9,8},{10,9},{11,10},{12... | collective-permute-start | bytes 3538952 | tf_op jit(solution)/shard_map/ppermute | solution.py:19
  21.5 1.0 slice.257
  22.5 5.3 %fusion.80 = (f32[9,32,8,511]{3,1,2,0:T(8,128)}, f32[9,32,8,511]{3,1,2,0:T(8,128)}) fusion(f32[9,32,8,512]{3,1,2,0:T(8,128)S(1)} %copy_multiply_fusion), kind=kLoop, calls=%fused_computation.149 | loop fusion | bytes 18837504 | tf_op jit(solution)/shard_map/jit(_roll_static)/slice | solution.py:61
  27.8 1.5 fusion.81
  29.3 3.4 %slice.263 = f32[9,32,8,510]{3,1,2,0:T(8,128)} slice(f32[9,32,8,512]{3,1,2,0:T(8,128)S(1)} %copy_multiply_fusion), slice={[0:9], [0:32], [0:8], [2:512]} | slice | bytes 9400320 | tf_op jit(solution)/shard_map/jit(_roll_static)/slice | solution.py:62
  32.7 0.2 slice.264
  33.0 1.3 maximum_minimum_fusion
  34.2 0.0 copy-start.7
  34.3 13.0 %multiply_multiply_fusion.4 = f32[9,32,8,512]{3,1,2,0:T(8,128)} fusion(f32[9,32,8,511]{3,1,2,0:T(8,128)} %get-tuple-element.19, f32[9,32,8,1]{3,1,2,0:T(8,128)} %get-tuple-element.21, f32[9,32,8,2]{3,1,2,0:T(8,128)S(1)} %slice.264, f32[9,32,8,510]{3,1,2,0:T(8,128)} %slice.263, f32[9,32,8,1]{3,1,2,0:T(8,128)S(1)} %get-tuple-element.20, ...), kind=kLoop, calls=%fused_computation.6 | loop fusion | flops 36569088 | bytes 24133668 | tf_op jit(solution)/shard_map/mul | solution.py:50
  47.2 0.6 fusion.74
  48.5 0.6 multiply_exponential_fusion
  49.1 0.6 multiply_multiply_fusion.8
  49.7 0.6 fusion.70
  50.4 0.6 broadcast_divide_fusion
  50.9 1.6 slice.265
  52.6 0.6 slice_bitcast_fusion.3
  53.2 0.0 collective-permute-done
  53.2 0.0 slice-start
  53.2 0.0 slice-start.2
  53.2 1.1 fusion.66
  54.3 0.0 collective-permute-done.2
  54.3 0.0 slice-start.3
  54.3 10.9 %multiply_multiply_fusion.1 = f32[9,32,9,512]{3,1,2,0:T(8,128)S(1)} fusion(f32[9,32,2,512]{3,1,2,0:T(8,128)} %collective-permute-done.3, f32[9,32,8,512]{3,1,2,0:T(8,128)} %copy-done, f32[9,32,2,512]{3,1,2,0:T(8,128)} %collective-permute-done.2, f32[9]{0:T(128)S(1)} %get-tuple-element.38, f32[32,9,512]{2,0,1:T(8,128)S(1)} %fusion.66), kind=kLoop, calls=%fused_computation.1 | loop fusion | flops 41140224 | bytes 12976164 | tf_op jit(solution)/shard_map/mul | solution.py:50
  65.3 7.4 %fusion.63 = f32[9,32,8,512]{3,1,2,0:T(8,128)S(1)} fusion(f32[9,32,9,512]{3,1,2,0:T(8,128)S(1)} %multiply_multiply_fusion.1, f32[9,32,8,512]{3,1,2,0:T(8,128)S(1)} %bitcast.19, f32[9,32,8,511]{3,1,2,0:T(8,128)S(1)} %bitcast.20, f32[9,32,8,1]{3,1,2,0:T(8,128)S(1)} %slice.265, f32[8,512]{1,0:T(8,128)S(1)} %convert_element_type.41, ...), kind=kLoop, calls=%fused_computation.96 | loop fusion | flops 7077888 | bytes 28327936 | tf_op jit(solution)/shard_map/sub | solution.py:76
  72.7 2.0 fusion.77
  74.7 1.3 slice.281
  76.0 0.5 fusion.78
  76.4 0.2 slice.282
  76.6 0.3 fusion.79
  76.9 2.7 %collective-permute-start.4 = (f32[9,32,2,512]{3,1,2,0:T(8,128)S(1)}, f32[9,32,2,512]{3,1,2,0:T(8,128)S(1)}, u32[]{:S(2)}, u32[]{:S(2)}) collective-permute-start(f32[9,32,2,512]{3,1,2,0:T(8,128)S(1)} %get-tuple-element.16), channel_id=1, source_target_pairs={{0,1},{1,2},{2,3},{3,4},{4,5},{5,6},{6,7},{8,9},{9,10},{10,11},{11... | collective-permute-start | bytes 3538952 | tf_op jit(solution)/shard_map/ppermute | solution.py:16
  79.6 2.9 %collective-permute-start.5 = (f32[9,32,2,512]{3,1,2,0:T(8,128)S(1)}, f32[9,32,2,512]{3,1,2,0:T(8,128)S(1)}, u32[]{:S(2)}, u32[]{:S(2)}) collective-permute-start(f32[9,32,2,512]{3,1,2,0:T(8,128)S(1)} %get-tuple-element.17), channel_id=1, source_target_pairs={{1,0},{2,1},{3,2},{4,3},{5,4},{6,5},{7,6},{9,8},{10,9},{11,10},{12... | collective-permute-start | bytes 3538952 | tf_op jit(solution)/shard_map/ppermute | solution.py:19
  82.5 5.7 %multiply_multiply_fusion.3 = f32[9,32,8,512]{3,1,2,0:T(8,128)S(1)} fusion(f32[9,32,8,511]{3,1,2,0:T(8,128)S(1)} %get-tuple-element.13, f32[9,32,8,1]{3,1,2,0:T(8,128)S(1)} %get-tuple-element.15, f32[9,32,8,2]{3,1,2,0:T(8,128)S(1)} %slice.282, f32[9,32,8,510]{3,1,2,0:T(8,128)S(1)} %slice.281, f32[9,32,8,512]{3,1,2,0:T(8,128)S(1)} %fusion.63, ...), kind=kLoop, calls=%fused_computation.5 | loop fusion | flops 35389440 | bytes 24117284 | tf_op jit(solution)/shard_map/mul | solution.py:50
  88.2 0.4 slice.283
  88.6 5.8 %collective-permute-done.4 = f32[9,32,2,512]{3,1,2,0:T(8,128)S(1)} collective-permute-done((f32[9,32,2,512]{3,1,2,0:T(8,128)S(1)}, f32[9,32,2,512]{3,1,2,0:T(8,128)S(1)}, u32[]{:S(2)}, u32[]{:S(2)}) %collective-permute-start.4) | collective-permute-done | bytes 1179680 | tf_op jit(solution)/shard_map/ppermute | solution.py:16
  94.4 13.4 %collective-permute-done.5 = f32[9,32,2,512]{3,1,2,0:T(8,128)S(1)} collective-permute-done((f32[9,32,2,512]{3,1,2,0:T(8,128)S(1)}, f32[9,32,2,512]{3,1,2,0:T(8,128)S(1)}, u32[]{:S(2)}, u32[]{:S(2)}) %collective-permute-start.5) | collective-permute-done | bytes 1179680 | tf_op jit(solution)/shard_map/ppermute | solution.py:19
  107.8 5.0 %multiply_multiply_fusion = f32[9,32,9,512]{3,1,2,0:T(8,128)S(1)} fusion(f32[9,32,2,512]{3,1,2,0:T(8,128)S(1)} %collective-permute-done.5, f32[9,32,8,512]{3,1,2,0:T(8,128)S(1)} %fusion.63, f32[9,32,2,512]{3,1,2,0:T(8,128)S(1)} %collective-permute-done.4, f32[9]{0:T(128)S(1)} %get-tuple-element.38, f32[32,9,512]{2,0,1:T(8,128)S(1)} %copy-done.4), kind=kLoop, calls=%fused_computation | loop fusion | flops 41140224 | bytes 12976164 | tf_op jit(solution)/shard_map/mul | solution.py:50
  112.9 0.0 copy-start.8
  112.9 0.0 copy-start.11
  112.9 3.4 %fusion.62 = f32[9,32,8,512]{3,1,2,0:T(8,128)S(1)} fusion(f32[9,32,9,512]{3,1,2,0:T(8,128)S(1)} %multiply_multiply_fusion, f32[9,32,8,512]{3,1,2,0:T(8,128)S(1)} %fusion.63, f32[9,32,8,512]{3,1,2,0:T(8,128)S(1)} %multiply_multiply_fusion.3, f32[9,32,8,511]{3,1,2,0:T(8,128)S(1)} %bitcast.21, f32[9,32,8,1]{3,1,2,0:T(8,128)S(1)} %slice.283), kind=kLoop, calls=%fused_computation.94 | loop fusion | flops 5898240 | bytes 28311552 | tf_op jit(solution)/shard_map/sub | solution.py:76
  116.3 0.3 fusion.76
  116.6 1.6 collective-permute-start.6
  118.2 2.2 %collective-permute-start.7 = (f32[2,32,8,512]{3,1,2,0:T(8,128)S(1)}, f32[2,32,8,512]{3,1,2,0:T(8,128)S(1)}, u32[]{:S(2)}, u32[]{:S(2)}) collective-permute-start(f32[2,32,8,512]{3,1,2,0:T(8,128)S(1)} %get-tuple-element.11), channel_id=1, source_target_pairs={{8,0},{16,8},{24,16},{0,24},{9,1},{17,9},{25,17},{1,25},{10,2},{18... | collective-permute-start | bytes 3145736 | tf_op jit(solution)/shard_map/ppermute | solution.py:19
  120.4 0.1 multiply_add_fusion.1
  120.6 0.1 multiply_subtract_fusion
  120.7 1.1 multiply_multiply_fusion.6
  121.8 22.7 %collective-permute-done.6 = f32[2,32,8,512]{3,1,2,0:T(8,128)S(1)} collective-permute-done((f32[2,32,8,512]{3,1,2,0:T(8,128)S(1)}, f32[2,32,8,512]{3,1,2,0:T(8,128)S(1)}, u32[]{:S(2)}, u32[]{:S(2)}) %collective-permute-start.6) | collective-permute-done | bytes 1048608 | tf_op jit(solution)/shard_map/ppermute | solution.py:16
  144.5 20.9 %collective-permute-done.7 = f32[2,32,8,512]{3,1,2,0:T(8,128)S(1)} collective-permute-done((f32[2,32,8,512]{3,1,2,0:T(8,128)S(1)}, f32[2,32,8,512]{3,1,2,0:T(8,128)S(1)}, u32[]{:S(2)}, u32[]{:S(2)}) %collective-permute-start.7) | collective-permute-done | bytes 1048608 | tf_op jit(solution)/shard_map/ppermute | solution.py:19
  165.4 4.8 %fusion.35 = f32[10,32,8,512]{3,1,2,0:T(8,128)S(1)} fusion(f32[2,32,8,512]{3,1,2,0:T(8,128)S(1)} %collective-permute-done.7, f32[9,32,8,512]{3,1,2,0:T(8,128)S(1)} %fusion.62, f32[2,32,8,512]{3,1,2,0:T(8,128)S(1)} %collective-permute-done.6, f32[13,32,8,512]{3,1,2,0:T(8,128)S(1)} %multiply_multiply_fusion.6), kind=kLoop, calls=%fused_computation.63 | loop fusion | flops 41943040 | bytes 22544384 | tf_op jit(solution)/shard_map/mul | solution.py:50
  170.3 3.5 %multiply_reduce_fusion = (f32[8,512]{1,0:T(8,128)S(1)}, f32[8,512]{1,0:T(8,128)S(1)}, f32[9,32,8,512]{3,1,2,0:T(8,128)}) fusion(f32[32]{0:T(128)S(1)} %copy-done.10, f32[32]{0:T(128)S(1)} %copy-done.9, f32[9,32,8,512]{3,1,2,0:T(8,128)S(1)} %fusion.62, f32[10,32,8,512]{3,1,2,0:T(8,128)S(1)} %fusion.35), kind=kLoop, calls=%fused_computation.109 | loop fusion | flops 7069696 | bytes 18907392 | tf_op jit(solution)/shard_map/reduce_sum | solution.py:136
  173.8 18.2 %all-reduce = (f32[8,512]{1,0:T(8,128)S(1)}, f32[8,512]{1,0:T(8,128)S(1)}) all-reduce(f32[8,512]{1,0:T(8,128)S(1)} %get-tuple-element.6, f32[8,512]{1,0:T(8,128)S(1)} %get-tuple-element.5), channel_id=1, replica_groups=mesh['comp'=4,'space'=8] {'comp'}, use_global_device_ids=true, to_apply=%region_2.3 | all-reduce | flops 8192 | bytes 65536 | tf_op jit(solution)/shard_map/psum | solution.py:135
  192.0 0.1 multiply_add_fusion
  192.2 3.6 %divide_multiply_fusion = f32[9,32,8,512]{3,1,2,0:T(8,128)S(1)} fusion(f32[9,32,8,512]{3,1,2,0:T(8,128)} %get-tuple-element.9, f32[32,8,512]{2,0,1:T(8,128)S(1)} %multiply_add_fusion, f32[32]{0:T(128)S(1)} %copy-done.9, f32[9,8,512]{2,1,0:T(8,128)S(1)} %multiply_add_fusion.1, f32[8,512]{1,0:T(8,128)S(1)} %convert_element_type.41), kind=kLoop, calls=%fused_computation.108 | loop fusion | flops 9437184 | bytes 10125440 | tf_op jit(solution)/shard_map/mul | solution.py:101
  195.8 4.9 %copy.9 = f32[9,32,8,512]{3,2,1,0:T(8,128)} copy(f32[9,32,8,512]{3,1,2,0:T(8,128)S(1)} %divide_multiply_fusion) | data formatting | bytes 9437184 | tf_op jit(solution)/shard_map/mul | solution.py:101
  (40 shorter events, 0.1 us)
Async XLA Ops:
  2.5 20.0 %copy-start.1 = (f32[32,8,512]{2,0,1:T(8,128)}, f32[32,8,512]{2,0,1:T(8,128)S(1)}, u32[]{:S(2)}) copy-start(f32[32,8,512]{2,0,1:T(8,128)S(1)} %add_multiply_fusion) | copy-start | bytes 1572868
  3.5 49.7 %collective-permute-start = (f32[32,4,512]{2,0,1:T(8,128)}, f32[32,4,512]{2,0,1:T(8,128)}, u32[]{:S(2)}, u32[]{:S(2)}) collective-permute-start(f32[32,4,512]{2,0,1:T(8,128)} %get-tuple-element.24), channel_id=1, source_target_pairs={{0,1},{1,2},{2,3},{3,4},{4,5},{5,6},{6,7},{8,9},{9,10},{10,11},{11... | collective-permute-start | bytes 786440 | tf_op jit(solution)/shard_map/ppermute | solution.py:16
  5.4 47.8 %collective-permute-start.1 = (f32[32,4,512]{2,0,1:T(8,128)}, f32[32,4,512]{2,0,1:T(8,128)}, u32[]{:S(2)}, u32[]{:S(2)}) collective-permute-start(f32[32,4,512]{2,0,1:T(8,128)} %get-tuple-element.25), channel_id=1, source_target_pairs={{1,0},{2,1},{3,2},{4,3},{5,4},{6,5},{7,6},{9,8},{10,9},{11,10},{12... | collective-permute-start | bytes 786440 | tf_op jit(solution)/shard_map/ppermute | solution.py:19
  14.2 18.6 %copy-start = (f32[9,32,8,512]{3,1,2,0:T(8,128)}, f32[9,32,8,512]{3,1,2,0:T(8,128)S(1)}, u32[]{:S(2)}) copy-start(f32[9,32,8,512]{3,1,2,0:T(8,128)S(1)} %copy_multiply_fusion) | copy-start | bytes 14155780
  15.9 38.4 %collective-permute-start.2 = (f32[9,32,2,512]{3,1,2,0:T(8,128)}, f32[9,32,2,512]{3,1,2,0:T(8,128)}, u32[]{:S(2)}, u32[]{:S(2)}) collective-permute-start(f32[9,32,2,512]{3,1,2,0:T(8,128)} %get-tuple-element.22), channel_id=1, source_target_pairs={{0,1},{1,2},{2,3},{3,4},{4,5},{5,6},{6,7},{8,9},{9,10},{10,11},{11... | collective-permute-start | bytes 3538952 | tf_op jit(solution)/shard_map/ppermute | solution.py:16
  17.9 36.5 %collective-permute-start.3 = (f32[9,32,2,512]{3,1,2,0:T(8,128)}, f32[9,32,2,512]{3,1,2,0:T(8,128)}, u32[]{:S(2)}, u32[]{:S(2)}) collective-permute-start(f32[9,32,2,512]{3,1,2,0:T(8,128)} %get-tuple-element.23), channel_id=1, source_target_pairs={{1,0},{2,1},{3,2},{4,3},{5,4},{6,5},{7,6},{9,8},{10,9},{11,10},{12... | collective-permute-start | bytes 3538952 | tf_op jit(solution)/shard_map/ppermute | solution.py:19
  29.3 3.6 %slice-start.4 = ((f32[32,8,512]{2,0,1:T(8,128)}), f32[32,8,1]{2,0,1:T(8,128)S(1)}, s32[]{:S(2)}) async-start(f32[32,8,512]{2,0,1:T(8,128)} %copy-done.1), calls=%async_computation.4 | async-start | bytes 262144 | tf_op jit(solution)/shard_map/jit(_roll_static)/slice | solution.py:57
  34.2 18.3 %copy-start.7 = (f32[2,8,512]{2,1,0:T(8,128)S(1)}, f32[2,8,512]{2,1,0:T(8,128)}, u32[]{:S(2)}) copy-start(f32[2,8,512]{2,1,0:T(8,128)} %param.11) | copy-start | bytes 98308
  34.3 18.9 %copy-start.2 = (f32[32,8,512]{2,0,1:T(8,128)S(1)}, f32[32,8,512]{2,0,1:T(8,128)}, u32[]{:S(2)}) copy-start(f32[32,8,512]{2,0,1:T(8,128)} %copy-done.1) | copy-start | bytes 1572868
  53.2 12.0 %slice-start = ((s8[4718592]{0:T(1024)(128)(4,1)}), s8[4194304]{0:T(1024)(128)(4,1)S(1)}, s32[]{:S(2)}) async-start(s8[4718592]{0:T(1024)(128)(4,1)} %bitcast.18), calls=%async_computation | async-start | bytes 8388608
  53.2 12.0 %slice-start.2 = ((s8[4718592]{0:T(1024)(128)(4,1)}), s8[4194304]{0:T(1024)(128)(4,1)S(1)}, s32[]{:S(2)}) async-start(s8[4718592]{0:T(1024)(128)(4,1)} %bitcast.22), calls=%async_computation.2 | async-start | bytes 8388608
  54.3 10.9 %copy-start.3 = (f32[32,9,512]{2,0,1:T(8,128)}, f32[32,9,512]{2,0,1:T(8,128)S(1)}, u32[]{:S(2)}) copy-start(f32[32,9,512]{2,0,1:T(8,128)S(1)} %fusion.66) | copy-start | bytes 1769476
  54.3 10.9 %slice-start.1 = ((s8[4718592]{0:T(1024)(128)(4,1)}), s8[524288]{0:T(1024)(128)(4,1)S(1)}, s32[]{:S(2)}) async-start(s8[4718592]{0:T(1024)(128)(4,1)} %bitcast.18), calls=%async_computation.1 | async-start | bytes 1048576
  54.3 10.9 %slice-start.3 = ((s8[4718592]{0:T(1024)(128)(4,1)}), s8[524288]{0:T(1024)(128)(4,1)S(1)}, s32[]{:S(2)}) async-start(s8[4718592]{0:T(1024)(128)(4,1)} %bitcast.22), calls=%async_computation.3 | async-start | bytes 1048576
  76.9 17.5 %collective-permute-start.4 = (f32[9,32,2,512]{3,1,2,0:T(8,128)S(1)}, f32[9,32,2,512]{3,1,2,0:T(8,128)S(1)}, u32[]{:S(2)}, u32[]{:S(2)}) collective-permute-start(f32[9,32,2,512]{3,1,2,0:T(8,128)S(1)} %get-tuple-element.16), channel_id=1, source_target_pairs={{0,1},{1,2},{2,3},{3,4},{4,5},{5,6},{6,7},{8,9},{9,10},{10,11},{11... | collective-permute-start | bytes 3538952 | tf_op jit(solution)/shard_map/ppermute | solution.py:16
  79.6 28.3 %collective-permute-start.5 = (f32[9,32,2,512]{3,1,2,0:T(8,128)S(1)}, f32[9,32,2,512]{3,1,2,0:T(8,128)S(1)}, u32[]{:S(2)}, u32[]{:S(2)}) collective-permute-start(f32[9,32,2,512]{3,1,2,0:T(8,128)S(1)} %get-tuple-element.17), channel_id=1, source_target_pairs={{1,0},{2,1},{3,2},{4,3},{5,4},{6,5},{7,6},{9,8},{10,9},{11,10},{12... | collective-permute-start | bytes 3538952 | tf_op jit(solution)/shard_map/ppermute | solution.py:19
  82.4 25.4 %copy-start.4 = (f32[32,9,512]{2,0,1:T(8,128)S(1)}, f32[32,9,512]{2,0,1:T(8,128)}, u32[]{:S(2)}) copy-start(f32[32,9,512]{2,0,1:T(8,128)} %copy-done.3) | copy-start | bytes 1769476
  112.9 7.6 %copy-start.8 = (f32[2,8,512]{2,1,0:T(8,128)S(1)}, f32[2,8,512]{2,1,0:T(8,128)}, u32[]{:S(2)}) copy-start(f32[2,8,512]{2,1,0:T(8,128)} %param.13) | copy-start | bytes 98308
  112.9 7.7 %copy-start.5 = (f32[8,512]{1,0:T(8,128)S(1)}, f32[8,512]{1,0:T(8,128)}, u32[]{:S(2)}) copy-start(f32[8,512]{1,0:T(8,128)} %get-tuple-element.28) | copy-start | bytes 49156
  112.9 7.7 %copy-start.6 = (f32[8,512]{1,0:T(8,128)S(1)}, f32[8,512]{1,0:T(8,128)}, u32[]{:S(2)}) copy-start(f32[8,512]{1,0:T(8,128)} %get-tuple-element.29) | copy-start | bytes 49156
  112.9 7.7 %copy-start.13 = (f32[13]{0:T(128)S(1)}, f32[13]{0:T(128)}, u32[]{:S(2)}) copy-start(f32[13]{0:T(128)} %get-tuple-element.40) | copy-start | bytes 160
  112.9 7.7 %copy-start.14 = (f32[13]{0:T(128)S(1)}, f32[13]{0:T(128)}, u32[]{:S(2)}) copy-start(f32[13]{0:T(128)} %get-tuple-element.41) | copy-start | bytes 160
  112.9 7.8 %copy-start.11 = (f32[32]{0:T(128)S(1)}, f32[32]{0:T(128)}, u32[]{:S(2)}) copy-start(f32[32]{0:T(128)} %param.12) | copy-start | bytes 388
  116.6 27.9 %collective-permute-start.6 = (f32[2,32,8,512]{3,1,2,0:T(8,128)S(1)}, f32[2,32,8,512]{3,1,2,0:T(8,128)S(1)}, u32[]{:S(2)}, u32[]{:S(2)}) collective-permute-start(f32[2,32,8,512]{3,1,2,0:T(8,128)S(1)} %get-tuple-element.10), channel_id=1, source_target_pairs={{0,8},{8,16},{16,24},{24,0},{1,9},{9,17},{17,25},{25,1},{2,10},{10... | collective-permute-start | bytes 3145736 | tf_op jit(solution)/shard_map/ppermute | solution.py:16
  118.2 47.2 %collective-permute-start.7 = (f32[2,32,8,512]{3,1,2,0:T(8,128)S(1)}, f32[2,32,8,512]{3,1,2,0:T(8,128)S(1)}, u32[]{:S(2)}, u32[]{:S(2)}) collective-permute-start(f32[2,32,8,512]{3,1,2,0:T(8,128)S(1)} %get-tuple-element.11), channel_id=1, source_target_pairs={{8,0},{16,8},{24,16},{0,24},{9,1},{17,9},{25,17},{1,25},{10,2},{18... | collective-permute-start | bytes 3145736 | tf_op jit(solution)/shard_map/ppermute | solution.py:19
  121.8 48.5 %copy-start.9 = (f32[32]{0:T(128)S(1)}, f32[32]{0:T(128)}, u32[]{:S(2)}) copy-start(f32[32]{0:T(128)} %multiply_exponential_fusion) | copy-start | bytes 388
  121.8 48.5 %copy-start.10 = (f32[32]{0:T(128)S(1)}, f32[32]{0:T(128)}, u32[]{:S(2)}) copy-start(f32[32]{0:T(128)} %broadcast_divide_fusion) | copy-start | bytes 388
  170.2 21.8 %copy-start.12 = (f32[32]{0:T(128)S(1)}, f32[32]{0:T(128)}, u32[]{:S(2)}) copy-start(f32[32]{0:T(128)} %multiply_multiply_fusion.8) | copy-start | bytes 388
where the time goes:
time: 201 us
  other arithmetic  70.9 us (35%)
  waiting for transfers between devices  62.9 us (31%)
  local copies, waits for them, and re-layouts  27 us (13%)
  starting transfers between devices  20.5 us (10%)
  blocking collectives  18.2 us (9%)
    mul x5, other arithmetic, quick_flux(): return courant * jnp.where(courant >= 0.0, rightward, leftward)  39.4 us
    ppermute x4, waiting for transfers between devices, with_halo(): lax.ppermute(lax.slice_in_dim(block, 0, width, axis=dim), axis, backward)  34.4 us
    ppermute x4, waiting for transfers between devices, with_halo(): lax.ppermute(lax.slice_in_dim(block, block.shape[dim] - width, None, axis...  28.5 us
    psum x1, blocking collectives, local(): lax.psum((jnp.sum(weighted, axis=(0, 1)), jnp.sum(weighted * freq_scale,...  18.2 us
    ppermute x4, starting transfers between devices, with_halo(): lax.ppermute(lax.slice_in_dim(block, 0, width, axis=dim), axis, backward)  12.4 us
    sub x2, other arithmetic, advect(): centre - (flux_along - jnp.roll(flux_along, 1, -1))  10.7 us
    slice x4, local copies, waits for them, and re-layouts, advect(): jnp.roll(centre, -1, -1)  9.25 us
    ppermute x4, starting transfers between devices, with_halo(): lax.ppermute(lax.slice_in_dim(block, block.shape[dim] - width, None, axis...  8.13 us
  transfers between devices with their start and end apart: 8, of which 4 were waited for; matrix products, arithmetic and copies ran while one was open for 23% of the time, Pallas kernels for 0%

commit v1 on v0

v1 whole, which is shorter than its diff:
```python
import functools
import math

import jax
import jax.numpy as jnp
from jax import lax
from jax.experimental import pallas as pl
from jax.experimental.pallas import tpu as pltpu
from jax.sharding import PartitionSpec as P

MESH = pl.DeviceIdType.MESH
LANES = 8


def freq_ratio(frequencies):
    position = jnp.arange(frequencies).astype(jnp.float32)
    return jnp.exp((position - 0.5 * (frequencies - 1)) * math.log(1.1))


def upwind(courant, half, third, cell, ahead, behind):
    bend = ahead + (1.0 / 3.0 + third) * (behind - ahead)
    return courant * (cell + (0.5 - half) * bend)


def scaled(speed, factor):
    return speed * factor, speed * (0.5 * factor), speed * (factor * (1.0 / 3.0))


def kernel(
    dims, cos_ref, sin_ref, fsin_ref, fcos_ref, x_ref, code_ref, slope_ref, table_ref, gain_ref,
    wgt_ref, wgtr_ref, out_ref, sums_ref, code, speed, along, across, q0, q1, q2, zlo, zhi, turn, q3,
    acc, part, peers, code_s, code_r, h0_s, h0_r, h1_s, h1_r, z_s, z_r, e_s, e_r,
):
    groups, spaces, dirs, blocks, rows, cols = dims
    depths = table_ref.shape[0]
    me = lax.axis_index("comp")
    sp = lax.axis_index("space")
    southward = (2 * me) // groups
    westward = ((4 * me // groups + 1) // 2) % 2
    sgn = 1 - 2 * southward
    first = southward * (rows - 1)
    down = sp + sgn
    up = sp - sgn
    has_down = jnp.logical_and(down >= 0, down < spaces)
    has_up = jnp.logical_and(up >= 0, up < spaces)
    right = lax.rem(me + 1, groups)
    left = lax.rem(me + groups - 1, groups)

    barrier = pltpu.get_barrier_semaphore()
    for has, other in ((has_down, down), (has_up, up)):

        @pl.when(has)
        def _():
            pl.semaphore_signal(barrier, inc=1, device_id=(me, other), device_id_type=MESH)

    for step in range(1, groups):
        pl.semaphore_signal(
            barrier, inc=1, device_id=(lax.rem(me + step, groups), sp), device_id_type=MESH
        )

    land = jnp.full((LANES, cols), -1.0, jnp.float32)
    for r in range(rows):
        code[1 + first + sgn * r] = jnp.broadcast_to(code_ref[r : r + 1, :], (LANES, cols))

    @pl.when(jnp.logical_not(has_up))
    def _():
        code[0] = land
        for b in range(blocks):
            for q in (q0, q1):
                q[b, :, 0:2] = jnp.zeros((dirs, 2, LANES, cols), jnp.float32)

    @pl.when(jnp.logical_not(has_down))
    def _():
        code[rows + 1] = land
        for b in range(blocks):
            for q in (q0, q1):
                q[b, :, rows + 2 : rows + 3] = jnp.zeros((dirs, 1, LANES, cols), jnp.float32)

    pl.semaphore_wait(barrier, groups - 1 + has_down.astype(jnp.int32) + has_up.astype(jnp.int32))

    def remote(src, dst, ssem, rsem, target):
        return pltpu.make_async_remote_copy(
            src_ref=src, dst_ref=dst, send_sem=ssem, recv_sem=rsem, device_id=target,
            device_id_type=MESH,
        )

    code_copies = (
        remote(code.at[rows], code.at[0], code_s.at[0], code_r.at[0], (me, down)),
        remote(code.at[1], code.at[rows + 1], code_s.at[1], code_r.at[1], (me, up)),
    )
    parts = ((0, 4), (4, dirs - 4))

    def halo(q, ssem, rsem, part_no, b):
        start, count = parts[part_no]
        ks = pl.ds(start, count)
        return (
            remote(
                q.at[b, ks, pl.ds(rows, 2)], q.at[b, ks, pl.ds(0, 2)],
                ssem.at[part_no, b, 0], rsem.at[part_no, b, 0], (me, down),
            ),
            remote(
                q.at[b, ks, pl.ds(2, 1)], q.at[b, ks, pl.ds(rows + 2, 1)],
                ssem.at[part_no, b, 1], rsem.at[part_no, b, 1], (me, up),
            ),
        )

    def start(copies):
        pl.when(has_down)(copies[0].start)
        pl.when(has_up)(copies[1].start)

    def wait_recv(copies):
        pl.when(has_up)(copies[0].wait_recv)
        pl.when(has_down)(copies[1].wait_recv)

    def wait_send(copies):
        pl.when(has_down)(copies[0].wait_send)
        pl.when(has_up)(copies[1].wait_send)

    start(code_copies)

    def place(p, part_no):
        return p + (p // 2) * (dirs - 4) if part_no == 0 else p - 2

    def load(part_no):
        lo, count = parts[part_no]

        def block(b, _):
            def one(p, _):
                k = place(p, part_no)
                tile = x_ref[k, pl.ds(b * LANES, LANES)]
                tile = jnp.swapaxes(tile, 0, 1)
                for r in range(rows):
                    j = first + sgn * r
                    q0[b, p, 2 + j] = jnp.where(code[1 + j] >= 0.0, tile[r], 0.0)
                return 0

            lax.fori_loop(lo, lo + count, one, 0)
            start(halo(q0, h0_s, h0_r, part_no, b))
            return 0

        lax.fori_loop(0, blocks, block, 0)

    def shifts(west):
        ahead, back = (1, cols - 1) if west else (cols - 1, 1)
        return (lambda v: pltpu.roll(v, ahead, 1)), (lambda v: pltpu.roll(v, back, 1))

    def prepare(west):
        nxt, _ = shifts(west)

        def block(b, _):
            for j in range(rows + 2):
                now = code[j]
                value = jnp.zeros((LANES, cols), jnp.float32)
                for level in range(depths):
                    value = jnp.where(now == float(level), table_ref[level, b], value)
                speed[j] = value
            for j in range(rows):
                value = speed[1 + j]
                along[b, j] = jnp.minimum(value, nxt(value))
            for j in range(rows + 1):
                across[b, j] = jnp.minimum(speed[j], speed[j + 1])
            return 0

        lax.fori_loop(0, blocks, block, 0)

    def substep(west, src, b, p, write):
        nxt, prv = shifts(west)
        cosine = cos_ref[p]
        sine = sin_ref[p]
        behind = src[b, p, 1] - src[b, p, 0]
        cell = src[b, p, 1]
        flux_in = None
        for i in range(rows + 1):
            after = src[b, p, i + 2]
            ahead = after - cell
            flux = upwind(*scaled(across[b, i], sine), cell, ahead, behind)
            if i > 0:
                step = nxt(cell) - cell
                fx = upwind(*scaled(along[b, i - 1], cosine), cell, step, prv(step))
                write(i - 1, cell - (fx - prv(fx)) - (flux - flux_in))
            flux_in = flux
            behind = ahead
            cell = after

    def first_pass(west, part_no):
        lo, count = parts[part_no]

        def block(b, _):
            wait_recv(halo(q0, h0_s, h0_r, part_no, b))

            def one(p, _):
                def write(j, value):
                    q1[b, p, 2 + j] = value

                substep(west, q0, b, p, write)
                return 0

            lax.fori_loop(lo, lo + count, one, 0)
            start(halo(q1, h1_s, h1_r, part_no, b))
            return 0

        lax.fori_loop(0, blocks, block, 0)

    def exchange(b):
        return (
            remote(
                q2.at[b, pl.ds(dirs - 2, 2)], zlo.at[b], z_s.at[b, 0], z_r.at[b, 0], (right, sp)
            ),
            remote(q2.at[b, pl.ds(0, 2)], zhi.at[b], z_s.at[b, 1], z_r.at[b, 1], (left, sp)),
        )

    def second_pass(west, part_no):
        lo, count = parts[part_no]

        def block(b, _):
            wait_recv(halo(q1, h1_s, h1_r, part_no, b))

            def one(p, _):
                k = place(p, part_no)

                def write(j, value):
                    q2[b, k, first + sgn * j] = value

                substep(west, q1, b, p, write)
                return 0

            lax.fori_loop(lo, lo + count, one, 0)
            if part_no == 0:
                for copy in exchange(b):
                    copy.start()
            return 0

        lax.fori_loop(0, blocks, block, 0)

    def both(fn):
        @pl.when(westward == 0)
        def _():
            fn(False)

        @pl.when(westward == 1)
        def _():
            fn(True)

    load(0)
    wait_recv(code_copies)

    def stage(west):
        prepare(west)
        first_pass(west, 0)
        load(1)
        second_pass(west, 0)
        first_pass(west, 1)

    both(stage)

    for face in range(dirs + 1):
        rate = fsin_ref[face] * slope_ref[0] - fcos_ref[face] * slope_ref[1]
        rate = jnp.where(code_ref[...] >= 0.0, rate, 0.0)
        for r in range(rows):
            turn[face, r] = jnp.broadcast_to(rate[r : r + 1, :], (LANES, cols))

    both(lambda west: second_pass(west, 1))

    acc[...] = jnp.zeros(acc.shape, jnp.float32)

    def refract(b, _):
        for copy in exchange(b):
            copy.wait_recv()
        gain = gain_ref[b]

        def row(r, _):
            def wave(k):
                if k < 0:
                    return zlo[b, k + 2, r]
                if k >= dirs:
                    return zhi[b, k - dirs, r]
                return q2[b, k, r]

            total = jnp.zeros((LANES, cols), jnp.float32)
            before, here, after = wave(-2), wave(-1), wave(0)
            d_left, d_mid = here - before, after - here
            flux_in = None
            for face in range(dirs + 1):
                beyond = wave(face + 1)
                d_right = beyond - after
                courant = gain * turn[face, r]
                size = jnp.abs(courant)
                positive = courant >= 0.0
                bend = d_mid + (1.0 / 3.0 + size * (1.0 / 3.0)) * (
                    jnp.where(positive, d_left, d_right) - d_mid
                )
                bend = bend * (0.5 - 0.5 * size)
                flux = courant * jnp.where(positive, here + bend, after - bend)
                if face > 0:
                    value = here - (flux - flux_in)
                    q3[face - 1, r] = value
                    total = total + value
                flux_in = flux
                here, after = after, beyond
                d_left, d_mid = d_mid, d_right
            acc[0, r] += total * wgt_ref[b]
            acc[1, r] += total * wgtr_ref[b]
            return 0

        lax.fori_loop(0, rows, row, 0)

        def put(k, _):
            out_ref[k, pl.ds(b * LANES, LANES)] = jnp.swapaxes(q3[k], 0, 1)
            return 0

        lax.fori_loop(0, dirs, put, 0)
        return 0

    lax.fori_loop(0, blocks, refract, 0)

    for m in range(2):
        part[m] = jnp.sum(acc[m], axis=1)
    sums = [
        remote(part, peers.at[step - 1], e_s.at[step - 1], e_r.at[step - 1],
               (lax.rem(me + step, groups), sp))
        for step in range(1, groups)
    ]
    for copy in sums:
        copy.start()

    wait_send(code_copies)

    def drain(b, _):
        for part_no in range(2):
            wait_send(halo(q0, h0_s, h0_r, part_no, b))
            wait_send(halo(q1, h1_s, h1_r, part_no, b))
        for copy in exchange(b):
            copy.wait_send()
        return 0

    lax.fori_loop(0, blocks, drain, 0)
    total = part[...]
    for step, copy in enumerate(sums):
        copy.wait()
        total = total + peers[step]
    sums_ref[...] = total


def local(spectrum, sea_mask, depth_class, speed_table, depth_slope, turn_gain, wind_vector):
    dirs, freqs, rows, cols = spectrum.shape
    groups = lax.axis_size("comp")
    spaces = lax.axis_size("space")
    assert groups % 4 == 0 and freqs % LANES == 0 and dirs > 4
    all_dirs = dirs * groups
    blocks = freqs // LANES
    offset = lax.axis_index("comp") * dirs
    step_angle = 2.0 * math.pi / all_dirs
    angles = ((offset + jnp.arange(dirs)).astype(jnp.float32) + 0.5) * step_angle
    cosine, sine_dir = jnp.cos(angles), jnp.sin(angles)
    places = jnp.array([0, 1, dirs - 2, dirs - 1] + list(range(2, dirs - 2)))
    ext = ((offset - 1 + jnp.arange(dirs + 2)).astype(jnp.float32) + 0.5) * step_angle
    ext_s, ext_c = jnp.sin(ext), jnp.cos(ext)
    face_s, face_c = 0.5 * (ext_s[1:] + ext_s[:-1]), 0.5 * (ext_c[1:] + ext_c[:-1])
    code = jnp.where(sea_mask > 0, depth_class, -1).astype(jnp.float32)
    ratios = freq_ratio(freqs)
    weights = ratios / (all_dirs * jnp.sum(ratios))

    def spread(v):
        shape = v.shape[:-1] + (blocks, LANES, cols)
        return jnp.broadcast_to(v.reshape(v.shape[:-1] + (blocks, LANES, 1)), shape)

    vmem = pl.BlockSpec(memory_space=pltpu.VMEM)
    smem = pl.BlockSpec(memory_space=pltpu.SMEM)
    f32 = jnp.float32
    tile = (LANES, cols)
    dma = pltpu.SemaphoreType.DMA
    waves, (energy, moment) = pl.pallas_call(
        functools.partial(kernel, (groups, spaces, dirs, blocks, rows, cols)),
        out_shape=(
            jax.ShapeDtypeStruct(spectrum.shape, f32),
            jax.ShapeDtypeStruct((2, rows, cols), f32),
        ),
        in_specs=[smem] * 4 + [vmem] * 7,
        out_specs=(vmem, vmem),
        scratch_shapes=[
            pltpu.VMEM((rows + 2,) + tile, f32),
            pltpu.VMEM((rows + 2,) + tile, f32),
            pltpu.VMEM((blocks, rows) + tile, f32),
            pltpu.VMEM((blocks, rows + 1) + tile, f32),
            pltpu.VMEM((blocks, dirs, rows + 3) + tile, f32),
            pltpu.VMEM((blocks, dirs, rows + 3) + tile, f32),
            pltpu.VMEM((blocks, dirs, rows) + tile, f32),
            pltpu.VMEM((blocks, 2, rows) + tile, f32),
            pltpu.VMEM((blocks, 2, rows) + tile, f32),
            pltpu.VMEM((dirs + 1, rows) + tile, f32),
            pltpu.VMEM((dirs, rows) + tile, f32),
            pltpu.VMEM((2, rows) + tile, f32),
            pltpu.VMEM((2, rows, cols), f32),
            pltpu.VMEM((groups - 1, 2, rows, cols), f32),
            dma((2,)), dma((2,)),
            dma((2, blocks, 2)), dma((2, blocks, 2)),
            dma((2, blocks, 2)), dma((2, blocks, 2)),
            dma((blocks, 2)), dma((blocks, 2)),
            dma((groups - 1,)), dma((groups - 1,)),
        ],
        compiler_params=pltpu.CompilerParams(
            collective_id=0, has_side_effects=True, vmem_limit_bytes=52 * 1024 * 1024
        ),
    )(
        jnp.abs(cosine[places]), jnp.abs(sine_dir[places]), face_s, face_c,
        spectrum, code, depth_slope, spread(speed_table), spread(turn_gain),
        spread(weights), spread(weights * ratios),
    )
    wet_mask = sea_mask.astype(f32)
    mean_freq = moment / jnp.maximum(energy, 0.25)
    steepness = energy * mean_freq * mean_freq / 4.0
    strength = 0.25 * steepness * steepness / jnp.maximum(mean_freq, 0.5)
    scale = ratios[None, :, None, None]
    cos4, sin4 = cosine[:, None, None, None], sine_dir[:, None, None, None]
    projected = wind_vector[0] * cos4 + wind_vector[1] * sin4
    growth = 0.2 * jnp.maximum(projected * scale - 1.0, 0.0)
    return waves * (1.0 + growth) / (1.0 + scale * scale * strength) * wet_mask


def solution(mesh):
    in_specs = (
        P("comp", None, "space", None),
        P("space", None),
        P("space", None),
        P(),
        P(None, "space", None),
        P(),
        P(None, "space", None),
    )
    out_specs = P("comp", None, "space", None)
    return jax.shard_map(local, mesh=mesh, in_specs=in_specs, out_specs=out_specs, check_vma=False)
```

time: 201 us -> 86.4 us (0.43)
  Pallas kernels: 0 us -> 70.9 us
  waiting for transfers between devices: 62.9 us -> 0 us
  other arithmetic: 70.9 us -> 8.4 us
  local copies, waits for them, and re-layouts: 27 us -> 4.61 us
  starting transfers between devices: 20.5 us -> 0 us
  blocking collectives: 18.2 us -> 0 us
    pallas_call x0 -> x1, Pallas kernels: none -> 70.9 us  [local(): pl.pallas_call(functools.partial(kernel, (groups, spaces, dirs, blocks, r...]
    ppermute x8 -> x0, waiting for transfers between devices: 62.9 us -> none  [the longest x4 34.4 us: with_halo(): lax.ppermute(lax.slice_in_dim(block, 0, width, axis=dim), axis, backward)]
    mul x10 -> x5, other arithmetic: 50 us -> 6 us  [the longest x2 5.84 us: local(): return waves * (1.0 + growth) / (1.0 + scale * scale * strength) * wet_mask]
    ppermute x8 -> x0, starting transfers between devices: 20.5 us -> none  [the longest x4 12.4 us: with_halo(): lax.ppermute(lax.slice_in_dim(block, 0, width, axis=dim), axis, backward)]
    slice x17 -> x0, local copies, waits for them, and re-layouts: 20.5 us -> none  [the longest x4 9.25 us: advect(): jnp.roll(centre, -1, -1)]
    psum x1 -> x0, blocking collectives: 18.2 us -> none  [local(): lax.psum((jnp.sum(weighted, axis=(0, 1)), jnp.sum(weighted * freq_scale,...]
    sub x3 -> x0, other arithmetic: 10.8 us -> none  [the longest x2 10.7 us: advect(): centre - (flux_along - jnp.roll(flux_along, 1, -1))]
    mul x4 -> x1, local copies, waits for them, and re-layouts: 6.35 us -> 0.74 us  [local(): projected = wind_vector[0] * cos4 + wind_vector[1] * sin4]
  transfers between devices with their start and end apart: 8 -> 0, of which waited for: 4 -> 0; matrix products, arithmetic and copies ran while one was open for 23% -> 0% of each run, Pallas kernels for 0% -> 0%
where the time goes in v1:
time: 86.4 us; the launch traced here: 84.6 us
  Pallas kernels  70.9 us (82%)
  other arithmetic  8.4 us (10%)
  local copies, waits for them, and re-layouts  4.61 us (5%)
    pallas_call x1, Pallas kernels, local(): pl.pallas_call(functools.partial(kernel, (groups, spaces, dirs, blocks, r...  70.9 us
    mul x2, other arithmetic, local(): return waves * (1.0 + growth) / (1.0 + scale * scale * strength) * wet_mask  5.84 us
    broadcast_in_dim x6, local copies, waits for them, and re-layouts, spread(): return jnp.broadcast_to(v.reshape(v.shape[:-1] + (blocks, LANES, 1)), shape)  1.8 us

profile of v1, /device:TPU:2, one launch (start us, length us, event | category | flops | bytes accessed | tf_op | source)
XLA Modules:
  0.0 84.6 jit_solution(16887626917663525894)
XLA Ops:
  0.0 0.6 fusion.7
  1.4 0.1 add_multiply_fusion.fcos_ref
  1.5 0.1 add_multiply_fusion.1.fsin_ref
  1.5 0.7 broadcast_in_dim.41
  2.3 0.7 pad_clamp_fusion
  3.0 0.7 gather_fusion.1
  3.6 0.7 gather_fusion
  4.3 0.8 broadcast_in_dim.20
  5.1 0.8 fusion.8
  5.9 0.7 slice_bitcast_fusion.1
  6.6 0.1 broadcast_in_dim.44.wgtr_ref
  6.7 0.1 broadcast_in_dim.42.gain_ref
  6.8 0.1 broadcast_in_dim.43.wgt_ref
  6.8 0.1 multiply_add_fusion.1
  6.9 0.1 broadcast_in_dim.40.table_ref
  7.0 0.0 copy-start
  7.0 0.7 copy-done
  7.8 70.9 %shard_map.82 = (f32[9,32,8,512]{3,2,1,0:T(8,128)}, f32[2,8,512]{2,1,0:T(8,128)S(1)}) custom-call(f32[9]{0:T(128)S(1)} %abs.6.cos_ref, f32[9]{0:T(128)S(1)} %abs.7.sin_ref, f32[10]{0:T(128)S(1)} %add_multiply_fusion.1.fsin_ref, f32[10]{0:T(128)S(1)} %add_multiply_fusion.fcos_ref, f32[9,32,8,512]{3,2,1,0:T(8,128)} %x_ref.1, ...), custom_call_target="tpu_custom_call" | custom-call | tf_op jit(solution)/shard_map/pallas_call | solution.py:372
  78.7 0.1 multiply_add_fusion
  78.8 5.8 %divide_multiply_fusion = f32[9,32,8,512]{3,2,1,0:T(8,128)} fusion(f32[9,32,8,512]{3,2,1,0:T(8,128)} %get-tuple-element.7, f32[8,512]{1,0:T(8,128)S(1)} %get-tuple-element.11, f32[32,8,512]{2,1,0:T(8,128)S(1)} %multiply_add_fusion, f32[32]{0:T(128)S(1)} %multiply_exponential_fusion.1, f32[9,8,512]{2,1,0:T(8,128)S(1)} %multiply_add_fusion.1), kind=kLoop, calls=%fused_computation.2 | loop fusion | flops 9437184 | bytes 10125440 | tf_op jit(solution)/shard_map/mul | solution.py:417
  (8 shorter events, 0.1 us)
Async XLA Ops:
  7.0 0.8 copy-start

commit v2 on v1

--- a/solution.py
+++ b/solution.py
@@ -3,6 +3,7 @@
 
 import jax
 import jax.numpy as jnp
+import numpy as np
 from jax import lax
 from jax.experimental import pallas as pl
 from jax.experimental.pallas import tpu as pltpu
@@ -12,9 +13,16 @@
 LANES = 8
 
 
-def freq_ratio(frequencies):
-    position = jnp.arange(frequencies).astype(jnp.float32)
-    return jnp.exp((position - 0.5 * (frequencies - 1)) * math.log(1.1))
+def ratio_list(frequencies):
+    return [math.exp((f - 0.5 * (frequencies - 1)) * math.log(1.1)) for f in range(frequencies)]
+
+
+def circle(all_dirs):
+    angles = (np.arange(all_dirs + 1) + 0.5) * (2.0 * math.pi / all_dirs)
+    cosine, sine = np.cos(angles), np.sin(angles)
+    before = angles - 2.0 * math.pi / all_dirs
+    face_c, face_s = 0.5 * (cosine + np.cos(before)), 0.5 * (sine + np.sin(before))
+    return np.concatenate([cosine, sine, face_c, face_s]).astype(np.float32)
 
 
 def upwind(courant, half, third, cell, ahead, behind):
@@ -27,12 +35,13 @@
 
 
 def kernel(
-    dims, cos_ref, sin_ref, fsin_ref, fcos_ref, x_ref, code_ref, slope_ref, table_ref, gain_ref,
-    wgt_ref, wgtr_ref, out_ref, sums_ref, code, speed, along, across, q0, q1, q2, zlo, zhi, turn, q3,
-    acc, part, peers, code_s, code_r, h0_s, h0_r, h1_s, h1_r, z_s, z_r, e_s, e_r,
+    dims, circle_ref, x_ref, mask_ref, class_ref, slope_ref, table_ref, gain_ref, out_ref, sums_ref,
+    code, lanes, speed, along, across, q0, q1, q2, zlo, zhi, turn, q3, acc, part, peers, code_s, code_r, h0_s, h0_r, h1_s, h1_r, z_s, z_r, e_s, e_r,
 ):
     groups, spaces, dirs, blocks, rows, cols = dims
-    depths = table_ref.shape[0]
+    depths, freqs = table_ref.shape
+    all_dirs = dirs * groups
+    weight_sum = all_dirs * sum(ratio_list(freqs))
     me = lax.axis_index("comp")
     sp = lax.axis_index("space")
     southward = (2 * me) // groups
@@ -59,8 +68,9 @@
         )
 
     land = jnp.full((LANES, cols), -1.0, jnp.float32)
+    coded = jnp.where(mask_ref[...] > 0, class_ref[...], -1).astype(jnp.float32)
     for r in range(rows):
-        code[1 + first + sgn * r] = jnp.broadcast_to(code_ref[r : r + 1, :], (LANES, cols))
+        code[1 + first + sgn * r] = jnp.broadcast_to(coded[r : r + 1, :], (LANES, cols))
 
     @pl.when(jnp.logical_not(has_up))
     def _():
@@ -124,7 +134,7 @@
     def load(part_no):
         lo, count = parts[part_no]
 
-        def block(b, _):
+        def block(b):
             def one(p, _):
                 k = place(p, part_no)
                 tile = x_ref[k, pl.ds(b * LANES, LANES)]
@@ -136,9 +146,8 @@
 
             lax.fori_loop(lo, lo + count, one, 0)
             start(halo(q0, h0_s, h0_r, part_no, b))
-            return 0
-
-        lax.fori_loop(0, blocks, block, 0)
+
+        return block
 
     def shifts(west):
         ahead, back = (1, cols - 1) if west else (cols - 1, 1)
@@ -146,13 +155,20 @@
 
     def prepare(west):
         nxt, _ = shifts(west)
+        own = lax.broadcasted_iota(jnp.int32, (freqs, freqs), 0)
+        other = lax.broadcasted_iota(jnp.int32, (freqs, freqs), 1)
+        for level in range(depths + 1):
+            line = table_ref[level : level + 1, :] if level < depths else gain_ref[...]
+            spread = jnp.where(own == other, jnp.broadcast_to(line, (freqs, freqs)), 0.0)
+            column = jnp.sum(spread, axis=1, keepdims=True)
+            lanes[level] = jnp.broadcast_to(column, (freqs, cols))
 
         def block(b, _):
             for j in range(rows + 2):
                 now = code[j]
                 value = jnp.zeros((LANES, cols), jnp.float32)
                 for level in range(depths):
-                    value = jnp.where(now == float(level), table_ref[level, b], value)
+                    value = jnp.where(now == float(level), lanes[level, pl.ds(b * LANES, LANES)], value)
                 speed[j] = value
             for j in range(rows):
                 value = speed[1 + j]
@@ -163,10 +179,10 @@
 
         lax.fori_loop(0, blocks, block, 0)
 
-    def substep(west, src, b, p, write):
+    def substep(west, src, b, p, k, write):
         nxt, prv = shifts(west)
-        cosine = cos_ref[p]
-        sine = sin_ref[p]
+        cosine = jnp.abs(circle_ref[me * dirs + k])
+        sine = jnp.abs(circle_ref[all_dirs + 1 + me * dirs + k])
         behind = src[b, p, 1] - src[b, p, 0]
         cell = src[b, p, 1]
         flux_in = None
@@ -185,21 +201,20 @@
     def first_pass(west, part_no):
         lo, count = parts[part_no]
 
-        def block(b, _):
+        def block(b):
             wait_recv(halo(q0, h0_s, h0_r, part_no, b))
 
             def one(p, _):
                 def write(j, value):
                     q1[b, p, 2 + j] = value
 
-                substep(west, q0, b, p, write)
+                substep(west, q0, b, p, place(p, part_no), write)
                 return 0
 
             lax.fori_loop(lo, lo + count, one, 0)
             start(halo(q1, h1_s, h1_r, part_no, b))
-            return 0
-
-        lax.fori_loop(0, blocks, block, 0)
+
+        return block
 
     def exchange(b):
         return (
@@ -212,7 +227,7 @@
     def second_pass(west, part_no):
         lo, count = parts[part_no]
 
-        def block(b, _):
+        def block(b):
             wait_recv(halo(q1, h1_s, h1_r, part_no, b))
 
             def one(p, _):
@@ -221,16 +236,15 @@
                 def write(j, value):
                     q2[b, k, first + sgn * j] = value
 
-                substep(west, q1, b, p, write)
+                substep(west, q1, b, p, k, write)
                 return 0
 
             lax.fori_loop(lo, lo + count, one, 0)
             if part_no == 0:
                 for copy in exchange(b):
                     copy.start()
-            return 0
-
-        lax.fori_loop(0, blocks, block, 0)
+
+        return block
 
     def both(fn):
         @pl.when(westward == 0)
@@ -241,32 +255,50 @@
         def _():
             fn(True)
 
-    load(0)
+    load(0)(0)
     wait_recv(code_copies)
 
     def stage(west):
         prepare(west)
-        first_pass(west, 0)
-        load(1)
-        second_pass(west, 0)
-        first_pass(west, 1)
-
-    both(stage)
+        jobs = ((1, load(0)), (0, first_pass(west, 0)), (0, load(1)), (-1, second_pass(west, 0)))
+
+        def step(s, _):
+            for lag, job in jobs:
+
+                @pl.when(jnp.logical_and(s + lag >= 0, s + lag < blocks))
+                def _():
+                    job(s + lag)
+
+            return 0
+
+        lax.fori_loop(0, blocks + 1, step, 0)
+
+        def inner(s, _):
+            pl.when(s < blocks)(lambda: first_pass(west, 1)(s))
+            pl.when(s > 0)(lambda: second_pass(west, 1)(s - 1))
+            return 0
+
+        lax.fori_loop(0, blocks + 1, inner, 0)
 
     for face in range(dirs + 1):
-        rate = fsin_ref[face] * slope_ref[0] - fcos_ref[face] * slope_ref[1]
-        rate = jnp.where(code_ref[...] >= 0.0, rate, 0.0)
+        face_c = circle_ref[2 * (all_dirs + 1) + me * dirs + face]
+        face_s = circle_ref[3 * (all_dirs + 1) + me * dirs + face]
+        rate = face_s * slope_ref[0] - face_c * slope_ref[1]
+        rate = jnp.where(mask_ref[...] > 0, rate, 0.0)
         for r in range(rows):
             turn[face, r] = jnp.broadcast_to(rate[r : r + 1, :], (LANES, cols))
 
-    both(lambda west: second_pass(west, 1))
+    both(stage)
 
     acc[...] = jnp.zeros(acc.shape, jnp.float32)
 
     def refract(b, _):
         for copy in exchange(b):
             copy.wait_recv()
-        gain = gain_ref[b]
+        gain = lanes[depths, pl.ds(b * LANES, LANES)]
+        place_f = b * LANES + lax.broadcasted_iota(jnp.int32, (LANES, cols), 0)
+        ratio = jnp.exp((place_f.astype(jnp.float32) - 0.5 * (freqs - 1)) * math.log(1.1))
+        weight = ratio * (1.0 / weight_sum)
 
         def row(r, _):
             def wave(k):
@@ -298,8 +330,9 @@
                 flux_in = flux
                 here, after = after, beyond
                 d_left, d_mid = d_mid, d_right
-            acc[0, r] += total * wgt_ref[b]
-            acc[1, r] += total * wgtr_ref[b]
+            total = total * weight
+            acc[0, r] += total
+            acc[1, r] += total * ratio
             return 0
 
         lax.fori_loop(0, rows, row, 0)
@@ -341,6 +374,28 @@
     sums_ref[...] = total
 
 
+def sources(dims, circle_ref, q_ref, sums_ref, wind_ref, mask_ref, out_ref, factor):
+    dirs, all_dirs, freqs = dims
+    ratios = ratio_list(freqs)
+    k = pl.program_id(0)
+
+    @pl.when(k == 0)
+    def _():
+        energy, moment = sums_ref[0], sums_ref[1]
+        mean_freq = moment / jnp.maximum(energy, 0.25)
+        steepness = energy * mean_freq * mean_freq / 4.0
+        strength = 0.25 * (steepness * steepness / jnp.maximum(mean_freq, 0.5))
+        wet = mask_ref[...].astype(jnp.float32)
+        for f in range(freqs):
+            factor[f] = wet / (1.0 + (ratios[f] * ratios[f]) * strength)
+
+    at = lax.axis_index("comp") * dirs + k
+    projected = wind_ref[0] * circle_ref[at] + wind_ref[1] * circle_ref[all_dirs + 1 + at]
+    for f in range(freqs):
+        growth = 0.2 * jnp.maximum(projected * ratios[f] - 1.0, 0.0)
+        out_ref[0, f] = q_ref[0, f] * (1.0 + growth) * factor[f]
+
+
 def local(spectrum, sea_mask, depth_class, speed_table, depth_slope, turn_gain, wind_vector):
     dirs, freqs, rows, cols = spectrum.shape
     groups = lax.axis_size("comp")
@@ -348,37 +403,23 @@
     assert groups % 4 == 0 and freqs % LANES == 0 and dirs > 4
     all_dirs = dirs * groups
     blocks = freqs // LANES
-    offset = lax.axis_index("comp") * dirs
-    step_angle = 2.0 * math.pi / all_dirs
-    angles = ((offset + jnp.arange(dirs)).astype(jnp.float32) + 0.5) * step_angle
-    cosine, sine_dir = jnp.cos(angles), jnp.sin(angles)
-    places = jnp.array([0, 1, dirs - 2, dirs - 1] + list(range(2, dirs - 2)))
-    ext = ((offset - 1 + jnp.arange(dirs + 2)).astype(jnp.float32) + 0.5) * step_angle
-    ext_s, ext_c = jnp.sin(ext), jnp.cos(ext)
-    face_s, face_c = 0.5 * (ext_s[1:] + ext_s[:-1]), 0.5 * (ext_c[1:] + ext_c[:-1])
-    code = jnp.where(sea_mask > 0, depth_class, -1).astype(jnp.float32)
-    ratios = freq_ratio(freqs)
-    weights = ratios / (all_dirs * jnp.sum(ratios))
-
-    def spread(v):
-        shape = v.shape[:-1] + (blocks, LANES, cols)
-        return jnp.broadcast_to(v.reshape(v.shape[:-1] + (blocks, LANES, 1)), shape)
-
+    angles = jnp.asarray(circle(all_dirs))
     vmem = pl.BlockSpec(memory_space=pltpu.VMEM)
     smem = pl.BlockSpec(memory_space=pltpu.SMEM)
     f32 = jnp.float32
     tile = (LANES, cols)
     dma = pltpu.SemaphoreType.DMA
-    waves, (energy, moment) = pl.pallas_call(
+    waves, sums = pl.pallas_call(
         functools.partial(kernel, (groups, spaces, dirs, blocks, rows, cols)),
         out_shape=(
             jax.ShapeDtypeStruct(spectrum.shape, f32),
             jax.ShapeDtypeStruct((2, rows, cols), f32),
         ),
-        in_specs=[smem] * 4 + [vmem] * 7,
+        in_specs=[smem] + [vmem] * 6,
         out_specs=(vmem, vmem),
         scratch_shapes=[
             pltpu.VMEM((rows + 2,) + tile, f32),
+            pltpu.VMEM((speed_table.shape[0] + 1, freqs, cols), f32),
             pltpu.VMEM((rows + 2,) + tile, f32),
             pltpu.VMEM((blocks, rows) + tile, f32),
             pltpu.VMEM((blocks, rows + 1) + tile, f32),
@@ -402,19 +443,25 @@
             collective_id=0, has_side_effects=True, vmem_limit_bytes=52 * 1024 * 1024
         ),
     )(
-        jnp.abs(cosine[places]), jnp.abs(sine_dir[places]), face_s, face_c,
-        spectrum, code, depth_slope, spread(speed_table), spread(turn_gain),
-        spread(weights), spread(weights * ratios),
+        angles, spectrum, sea_mask, depth_class, depth_slope, speed_table,
+        turn_gain.reshape(1, freqs),
     )
-    wet_mask = sea_mask.astype(f32)
-    mean_freq = moment / jnp.maximum(energy, 0.25)
-    steepness = energy * mean_freq * mean_freq / 4.0
-    strength = 0.25 * steepness * steepness / jnp.maximum(mean_freq, 0.5)
-    scale = ratios[None, :, None, None]
-    cos4, sin4 = cosine[:, None, None, None], sine_dir[:, None, None, None]
-    projected = wind_vector[0] * cos4 + wind_vector[1] * sin4
-    growth = 0.2 * jnp.maximum(projected * scale - 1.0, 0.0)
-    return waves * (1.0 + growth) / (1.0 + scale * scale * strength) * wet_mask
+
+    def whole(shape):
+        return pl.BlockSpec(shape, lambda k: (0,) * len(shape))
+
+    plane = pl.BlockSpec((1, freqs, rows, cols), lambda k: (k, 0, 0, 0))
+    return pl.pallas_call(
+        functools.partial(sources, (dirs, all_dirs, freqs)),
+        grid=(dirs,),
+        out_shape=jax.ShapeDtypeStruct(spectrum.shape, f32),
+        in_specs=[
+            smem, plane, whole((2, rows, cols)), whole((2, rows, cols)), whole((rows, cols)),
+        ],
+        out_specs=plane,
+        scratch_shapes=[pltpu.VMEM((freqs, rows, cols), f32)],
+        compiler_params=pltpu.CompilerParams(vmem_limit_bytes=24 * 1024 * 1024),
+    )(angles, waves, sums, wind_vector, sea_mask)
 
 
 def solution(mesh):

time: 86.4 us -> 84.2 us (0.975); the launches traced: 84.6 us -> 83.9 us
  other arithmetic: 8.4 us -> 0 us
  Pallas kernels: 70.9 us -> 77.3 us
  local copies, waits for them, and re-layouts: 4.61 us -> 6.54 us
    mul x5 -> x0, other arithmetic: 6 us -> none  [the longest x2 5.84 us: local(): return waves * (1.0 + growth) / (1.0 + scale * scale * strength) * wet_mask]
    unnamed x2 -> x16, local copies, waits for them, and re-layouts: 0.75 us -> 6.54 us
    pallas_call x0 -> x1, Pallas kernels: none -> 5.38 us  [local(): pl.pallas_call(functools.partial(sources, (dirs, all_dirs, freqs)), grid=...]
    broadcast_in_dim x6 -> x0, local copies, waits for them, and re-layouts: 1.8 us -> none  [spread(): return jnp.broadcast_to(v.reshape(v.shape[:-1] + (blocks, LANES, 1)), shape)]
    gather x2 -> x0, local copies, waits for them, and re-layouts: 1.32 us -> none  [the longest x1 0.67 us: local(): cosine[places]]
    pallas_call x1, Pallas kernels: 70.9 us -> 71.9 us  [local(): pl.pallas_call(functools.partial(kernel, (groups, spaces, dirs, blocks, r...]
where the time goes in v2:
time: 84.2 us; the launch traced here: 83.9 us
  Pallas kernels  77.3 us (92%)
  local copies, waits for them, and re-layouts  6.54 us (8%)
    pallas_call x1, Pallas kernels, local(): pl.pallas_call(functools.partial(kernel, (groups, spaces, dirs, blocks, r...  71.9 us
    unnamed x16, local copies, waits for them, and re-layouts  6.54 us
    pallas_call x1, Pallas kernels, local(): pl.pallas_call(functools.partial(sources, (dirs, all_dirs, freqs)), grid=...  5.38 us

profile of v2, /device:TPU:2, one launch (start us, length us, event | category | flops | bytes accessed | tf_op | source)
XLA Modules:
  0.0 83.9 jit_solution(10840240476149149627)
XLA Ops:
  0.0 0.0 copy-start.1
  0.0 0.7 copy-done.1
  0.7 0.0 copy-start.2
  0.7 0.8 copy-done.2
  1.5 0.0 copy-start.4
  1.5 0.7 copy-done.4
  2.2 0.0 copy-start.5
  2.2 0.7 copy-done.5
  2.9 0.0 copy-start.6
  2.9 0.7 copy-done.6
  3.6 0.0 copy-start.7
  3.6 0.7 copy-done.7
  4.2 0.0 copy-start.3
  4.2 71.9 %shard_map.82 = (f32[9,32,8,512]{3,2,1,0:T(8,128)}, f32[2,8,512]{2,1,0:T(8,128)S(1)}) custom-call(f32[148]{0:T(256)S(1)} %copy-done.5, f32[9,32,8,512]{3,2,1,0:T(8,128)} %x_ref.1, s32[8,512]{1,0:T(8,128)S(1)} %copy-done.1, s32[8,512]{1,0:T(8,128)S(1)} %copy-done.4, f32[2,8,512]{2,1,0:T(8,128)S(1)} %copy-done.2, f32[4,32]{1,0:T(4,128)S(1)} %copy-done.6, ...), custom_call_target="tpu_custom_call" | custom-call | tf_op jit(solution)/shard_map/pallas_call | solution.py:412
  76.1 0.0 copy-done.3
  76.2 0.0 copy-start
  76.2 2.3 %copy-done = f32[9,32,8,512]{3,2,1,0:T(8,128)S(1)} copy-done((f32[9,32,8,512]{3,2,1,0:T(8,128)S(1)}, f32[9,32,8,512]{3,2,1,0:T(8,128)}, u32[]{:S(2)}) %copy-start) | copy-done | bytes 4718616
  78.5 5.4 %shard_map.83 = f32[9,32,8,512]{3,2,1,0:T(8,128)} custom-call(f32[148]{0:T(256)S(1)} %copy-done.5, f32[9,32,8,512]{3,2,1,0:T(8,128)S(1)} %copy-done, f32[2,8,512]{2,1,0:T(8,128)S(1)} %get-tuple-element.8.sums_ref, f32[2,8,512]{2,1,0:T(8,128)S(1)} %copy-done.3, s32[8,512]{1,0:T(8,128)S(1)} %copy-done.1), custom_call_target="tpu_custom_call" | custom-call | tf_op jit(solution)/shard_map/pallas_call | solution.py:454
Async XLA Ops:
  0.0 0.7 copy-start.1
  0.7 0.8 copy-start.2
  1.5 0.7 copy-start.4
  2.2 0.7 copy-start.5
  2.9 0.7 copy-start.6
  3.6 0.7 copy-start.7
  4.2 71.9 %copy-start.3 = (f32[2,8,512]{2,1,0:T(8,128)S(1)}, f32[2,8,512]{2,1,0:T(8,128)}, u32[]{:S(2)}) copy-start(f32[2,8,512]{2,1,0:T(8,128)} %wind_ref.1) | copy-start | bytes 98308
  76.2 2.3 %copy-start = (f32[9,32,8,512]{3,2,1,0:T(8,128)S(1)}, f32[9,32,8,512]{3,2,1,0:T(8,128)}, u32[]{:S(2)}) copy-start(f32[9,32,8,512]{3,2,1,0:T(8,128)} %get-tuple-element.7.q_ref) | copy-start | bytes 14155780

commit v3 on v2

--- a/solution.py
+++ b/solution.py
@@ -35,7 +35,8 @@
 
 
 def kernel(
-    dims, circle_ref, x_ref, mask_ref, class_ref, slope_ref, table_ref, gain_ref, out_ref, sums_ref,
+    dims, circle_ref, x_hbm, mask_hbm, class_hbm, slope_hbm, table_hbm, gain_hbm, out_hbm, sums_ref,
+    x_ref, mask_ref, class_ref, slope_ref, table_ref, gain_ref, out_ref, in_s, x_s, out_s,
     code, lanes, speed, along, across, q0, q1, q2, zlo, zhi, turn, q3, acc, part, peers, code_s, code_r, h0_s, h0_r, h1_s, h1_r, z_s, z_r, e_s, e_r,
 ):
     groups, spaces, dirs, blocks, rows, cols = dims
@@ -67,6 +68,40 @@
             barrier, inc=1, device_id=(lax.rem(me + step, groups), sp), device_id_type=MESH
         )
 
+    small = [
+        pltpu.make_async_copy(src, dst, in_s.at[i])
+        for i, (src, dst) in enumerate(
+            (
+                (mask_hbm, mask_ref), (class_hbm, class_ref), (table_hbm, table_ref),
+                (gain_hbm, gain_ref), (slope_hbm, slope_ref),
+            )
+        )
+    ]
+    ranges = (((0, 2), (dirs - 2, 2)), ((2, dirs - 4),))
+
+    def fetch(part_no, b):
+        return [
+            pltpu.make_async_copy(
+                x_hbm.at[pl.ds(k, n), pl.ds(b * LANES, LANES)], x_ref.at[b, pl.ds(k, n)],
+                x_s.at[2 * part_no + i, b],
+            )
+            for i, (k, n) in enumerate(ranges[part_no])
+        ]
+
+    def deliver(b):
+        return pltpu.make_async_copy(
+            out_ref.at[b], out_hbm.at[:, pl.ds(b * LANES, LANES)], out_s.at[b]
+        )
+
+    for copy in small:
+        copy.start()
+    for part_no in range(2):
+        for b in range(blocks):
+            for copy in fetch(part_no, b):
+                copy.start()
+    for copy in small:
+        copy.wait()
+
     land = jnp.full((LANES, cols), -1.0, jnp.float32)
     coded = jnp.where(mask_ref[...] > 0, class_ref[...], -1).astype(jnp.float32)
     for r in range(rows):
@@ -135,9 +170,12 @@
         lo, count = parts[part_no]
 
         def block(b):
+            for copy in fetch(part_no, b):
+                copy.wait()
+
             def one(p, _):
                 k = place(p, part_no)
-                tile = x_ref[k, pl.ds(b * LANES, LANES)]
+                tile = x_ref[b, k]
                 tile = jnp.swapaxes(tile, 0, 1)
                 for r in range(rows):
                     j = first + sgn * r
@@ -216,12 +254,19 @@
 
         return block
 
-    def exchange(b):
+    half = rows // 2
+
+    def exchange(b, h):
+        at = pl.ds(h * half, half)
         return (
             remote(
-                q2.at[b, pl.ds(dirs - 2, 2)], zlo.at[b], z_s.at[b, 0], z_r.at[b, 0], (right, sp)
+                q2.at[b, pl.ds(dirs - 2, 2), at], zlo.at[b, :, at],
+                z_s.at[b, h, 0], z_r.at[b, h, 0], (right, sp),
             ),
-            remote(q2.at[b, pl.ds(0, 2)], zhi.at[b], z_s.at[b, 1], z_r.at[b, 1], (left, sp)),
+            remote(
+                q2.at[b, pl.ds(0, 2), at], zhi.at[b, :, at],
+                z_s.at[b, h, 1], z_r.at[b, h, 1], (left, sp),
+            ),
         )
 
     def second_pass(west, part_no):
@@ -241,8 +286,9 @@
 
             lax.fori_loop(lo, lo + count, one, 0)
             if part_no == 0:
-                for copy in exchange(b):
-                    copy.start()
+                for h in range(2):
+                    for copy in exchange(b, h):
+                        copy.start()
 
         return block
 
@@ -293,8 +339,6 @@
     acc[...] = jnp.zeros(acc.shape, jnp.float32)
 
     def refract(b, _):
-        for copy in exchange(b):
-            copy.wait_recv()
         gain = lanes[depths, pl.ds(b * LANES, LANES)]
         place_f = b * LANES + lax.broadcasted_iota(jnp.int32, (LANES, cols), 0)
         ratio = jnp.exp((place_f.astype(jnp.float32) - 0.5 * (freqs - 1)) * math.log(1.1))
@@ -335,13 +379,20 @@
             acc[1, r] += total * ratio
             return 0
 
-        lax.fori_loop(0, rows, row, 0)
+        def piece(h, _):
+            for copy in exchange(b, h):
+                copy.wait_recv()
+            lax.fori_loop(h * half, (h + 1) * half, row, 0)
+            return 0
+
+        lax.fori_loop(0, 2, piece, 0)
 
         def put(k, _):
-            out_ref[k, pl.ds(b * LANES, LANES)] = jnp.swapaxes(q3[k], 0, 1)
+            out_ref[b, k] = jnp.swapaxes(q3[k], 0, 1)
             return 0
 
         lax.fori_loop(0, dirs, put, 0)
+        deliver(b).start()
         return 0
 
     lax.fori_loop(0, blocks, refract, 0)
@@ -362,8 +413,10 @@
         for part_no in range(2):
             wait_send(halo(q0, h0_s, h0_r, part_no, b))
             wait_send(halo(q1, h1_s, h1_r, part_no, b))
-        for copy in exchange(b):
-            copy.wait_send()
+        for h in range(2):
+            for copy in exchange(b, h):
+                copy.wait_send()
+        deliver(b).wait()
         return 0
 
     lax.fori_loop(0, blocks, drain, 0)
@@ -400,12 +453,13 @@
     dirs, freqs, rows, cols = spectrum.shape
     groups = lax.axis_size("comp")
     spaces = lax.axis_size("space")
-    assert groups % 4 == 0 and freqs % LANES == 0 and dirs > 4
+    assert groups % 4 == 0 and freqs % LANES == 0 and dirs > 4 and rows % 2 == 0
     all_dirs = dirs * groups
     blocks = freqs // LANES
     angles = jnp.asarray(circle(all_dirs))
     vmem = pl.BlockSpec(memory_space=pltpu.VMEM)
     smem = pl.BlockSpec(memory_space=pltpu.SMEM)
+    hbm = pl.BlockSpec(memory_space=pl.ANY)
     f32 = jnp.float32
     tile = (LANES, cols)
     dma = pltpu.SemaphoreType.DMA
@@ -415,9 +469,17 @@
             jax.ShapeDtypeStruct(spectrum.shape, f32),
             jax.ShapeDtypeStruct((2, rows, cols), f32),
         ),
-        in_specs=[smem] + [vmem] * 6,
-        out_specs=(vmem, vmem),
+        in_specs=[smem] + [hbm] * 6,
+        out_specs=(hbm, vmem),
         scratch_shapes=[
+            pltpu.VMEM((blocks, dirs, LANES, rows, cols), f32),
+            pltpu.VMEM((rows, cols), jnp.int32),
+            pltpu.VMEM((rows, cols), jnp.int32),
+            pltpu.VMEM((2, rows, cols), f32),
+            pltpu.VMEM(speed_table.shape, f32),
+            pltpu.VMEM((1, freqs), f32),
+            pltpu.VMEM((blocks, dirs, LANES, rows, cols), f32),
+            dma((5,)), dma((3, blocks)), dma((blocks,)),
             pltpu.VMEM((rows + 2,) + tile, f32),
             pltpu.VMEM((speed_table.shape[0] + 1, freqs, cols), f32),
             pltpu.VMEM((rows + 2,) + tile, f32),
@@ -436,11 +498,11 @@
             dma((2,)), dma((2,)),
             dma((2, blocks, 2)), dma((2, blocks, 2)),
             dma((2, blocks, 2)), dma((2, blocks, 2)),
-            dma((blocks, 2)), dma((blocks, 2)),
+            dma((blocks, 2, 2)), dma((blocks, 2, 2)),
             dma((groups - 1,)), dma((groups - 1,)),
         ],
         compiler_params=pltpu.CompilerParams(
-            collective_id=0, has_side_effects=True, vmem_limit_bytes=52 * 1024 * 1024
+            collective_id=0, has_side_effects=True, vmem_limit_bytes=60 * 1024 * 1024
         ),
     )(
         angles, spectrum, sea_mask, depth_class, depth_slope, speed_table,
@@ -460,7 +522,7 @@
         ],
         out_specs=plane,
         scratch_shapes=[pltpu.VMEM((freqs, rows, cols), f32)],
-        compiler_params=pltpu.CompilerParams(vmem_limit_bytes=24 * 1024 * 1024),
+        compiler_params=pltpu.CompilerParams(vmem_limit_bytes=60 * 1024 * 1024),
     )(angles, waves, sums, wind_vector, sea_mask)
 
 

time: 84.2 us -> 77 us (0.914)
  local copies, waits for them, and re-layouts: 6.54 us -> 0 us
    unnamed x16 -> x0, local copies, waits for them, and re-layouts: 6.54 us -> none
    pallas_call x1, Pallas kernels: 71.9 us -> 68.7 us  [local(): pl.pallas_call(functools.partial(kernel, (groups, spaces, dirs, blocks, r...]
    pallas_call x1, Pallas kernels: 5.38 us -> 8.02 us  [local(): pl.pallas_call(functools.partial(sources, (dirs, all_dirs, freqs)), grid=...]
where the time goes in v3:
time: 77 us; the launch traced here: 76.7 us
  Pallas kernels  76.7 us (100%)
    pallas_call x1, Pallas kernels, local(): pl.pallas_call(functools.partial(kernel, (groups, spaces, dirs, blocks, r...  68.7 us
    pallas_call x1, Pallas kernels, local(): pl.pallas_call(functools.partial(sources, (dirs, all_dirs, freqs)), grid=...  8.02 us

profile of v3, /device:TPU:2, one launch (start us, length us, event | category | flops | bytes accessed | tf_op | source)
XLA Modules:
  0.0 76.7 jit_solution(9979713475008922250)
XLA Ops:
  0.0 68.7 %shard_map.82 = (f32[9,32,8,512]{3,2,1,0:T(8,128)}, f32[2,8,512]{2,1,0:T(8,128)}) custom-call(f32[148]{0:T(256)} %constant.2.clone.circle_ref, f32[9,32,8,512]{3,2,1,0:T(8,128)} %x_hbm.1, s32[8,512]{1,0:T(8,128)} %mask_ref.1, s32[8,512]{1,0:T(8,128)} %class_hbm.1, f32[2,8,512]{2,1,0:T(8,128)} %slope_hbm.1, f32[4,32]{1,0:T(4,128)} %table_hbm.1, f32[1,32]{1,0:T(1,128)} %bitcast.1), custom_call_target="tpu_custom_call" | custom-call | tf_op jit(solution)/shard_map/pallas_call | solution.py:466
  68.7 8.0 %shard_map.83 = f32[9,32,8,512]{3,2,1,0:T(8,128)} custom-call(f32[148]{0:T(256)} %constant.2.clone.circle_ref, f32[9,32,8,512]{3,2,1,0:T(8,128)} %get-tuple-element.7.q_ref, f32[2,8,512]{2,1,0:T(8,128)} %get-tuple-element.8.sums_ref, f32[2,8,512]{2,1,0:T(8,128)} %wind_ref.1, s32[8,512]{1,0:T(8,128)} %mask_ref.1), custom_call_target="tpu_custom_call" | custom-call | tf_op jit(solution)/shard_map/pallas_call | solution.py:516

commit v4 on v3

--- a/solution.py
+++ b/solution.py
@@ -306,7 +306,7 @@
 
     def stage(west):
         prepare(west)
-        jobs = ((1, load(0)), (0, first_pass(west, 0)), (0, load(1)), (-1, second_pass(west, 0)))
+        jobs = ((1, load(0)), (0, first_pass(west, 0)), (-1, second_pass(west, 0)), (0, load(1)))
 
         def step(s, _):
             for lag, job in jobs:
@@ -427,26 +427,41 @@
     sums_ref[...] = total
 
 
-def sources(dims, circle_ref, q_ref, sums_ref, wind_ref, mask_ref, out_ref, factor):
+def sources(
+    dims, circle_ref, q_hbm, sums_ref, wind_ref, mask_ref, out_hbm, factor, q_ref, out_ref, in_s, out_s
+):
     dirs, all_dirs, freqs = dims
     ratios = ratio_list(freqs)
-    k = pl.program_id(0)
-
-    @pl.when(k == 0)
-    def _():
-        energy, moment = sums_ref[0], sums_ref[1]
-        mean_freq = moment / jnp.maximum(energy, 0.25)
-        steepness = energy * mean_freq * mean_freq / 4.0
-        strength = 0.25 * (steepness * steepness / jnp.maximum(mean_freq, 0.5))
-        wet = mask_ref[...].astype(jnp.float32)
+
+    def fetch(k):
+        return pltpu.make_async_copy(q_hbm.at[k], q_ref.at[k], in_s.at[k])
+
+    def deliver(k):
+        return pltpu.make_async_copy(out_ref.at[k], out_hbm.at[k], out_s.at[k])
+
+    for k in range(dirs):
+        fetch(k).start()
+    energy, moment = sums_ref[0], sums_ref[1]
+    mean_freq = moment / jnp.maximum(energy, 0.25)
+    steepness = energy * mean_freq * mean_freq / 4.0
+    strength = 0.25 * (steepness * steepness / jnp.maximum(mean_freq, 0.5))
+    wet = mask_ref[...].astype(jnp.float32)
+    for f in range(freqs):
+        factor[f] = wet / (1.0 + (ratios[f] * ratios[f]) * strength)
+
+    def one(k, _):
+        fetch(k).wait()
+        at = lax.axis_index("comp") * dirs + k
+        projected = wind_ref[0] * circle_ref[at] + wind_ref[1] * circle_ref[all_dirs + 1 + at]
         for f in range(freqs):
-            factor[f] = wet / (1.0 + (ratios[f] * ratios[f]) * strength)
-
-    at = lax.axis_index("comp") * dirs + k
-    projected = wind_ref[0] * circle_ref[at] + wind_ref[1] * circle_ref[all_dirs + 1 + at]
-    for f in range(freqs):
-        growth = 0.2 * jnp.maximum(projected * ratios[f] - 1.0, 0.0)
-        out_ref[0, f] = q_ref[0, f] * (1.0 + growth) * factor[f]
+            growth = 0.2 * jnp.maximum(projected * ratios[f] - 1.0, 0.0)
+            out_ref[k, f] = q_ref[k, f] * (1.0 + growth) * factor[f]
+        deliver(k).start()
+        return 0
+
+    lax.fori_loop(0, dirs, one, 0)
+    for k in range(dirs):
+        deliver(k).wait()
 
 
 def local(spectrum, sea_mask, depth_class, speed_table, depth_slope, turn_gain, wind_vector):
@@ -509,19 +524,15 @@
         turn_gain.reshape(1, freqs),
     )
 
-    def whole(shape):
-        return pl.BlockSpec(shape, lambda k: (0,) * len(shape))
-
-    plane = pl.BlockSpec((1, freqs, rows, cols), lambda k: (k, 0, 0, 0))
+    block = pltpu.VMEM((dirs, freqs, rows, cols), f32)
     return pl.pallas_call(
         functools.partial(sources, (dirs, all_dirs, freqs)),
-        grid=(dirs,),
         out_shape=jax.ShapeDtypeStruct(spectrum.shape, f32),
-        in_specs=[
-            smem, plane, whole((2, rows, cols)), whole((2, rows, cols)), whole((rows, cols)),
+        in_specs=[smem, hbm, vmem, vmem, vmem],
+        out_specs=hbm,
+        scratch_shapes=[
+            pltpu.VMEM((freqs, rows, cols), f32), block, block, dma((dirs,)), dma((dirs,)),
         ],
-        out_specs=plane,
-        scratch_shapes=[pltpu.VMEM((freqs, rows, cols), f32)],
         compiler_params=pltpu.CompilerParams(vmem_limit_bytes=60 * 1024 * 1024),
     )(angles, waves, sums, wind_vector, sea_mask)
 

time: 77 us -> 73.7 us (0.957)
  Pallas kernels: 76.7 us -> 73.5 us
    pallas_call x1, Pallas kernels: 8.02 us -> 4.78 us  [local(): pl.pallas_call(functools.partial(sources, (dirs, all_dirs, freqs)), out_s...]
where the time goes in v4:
time: 73.7 us; the launch traced here: 73.5 us
  Pallas kernels  73.5 us (100%)
    pallas_call x1, Pallas kernels, local(): pl.pallas_call(functools.partial(kernel, (groups, spaces, dirs, blocks, r...  68.7 us
    pallas_call x1, Pallas kernels, local(): pl.pallas_call(functools.partial(sources, (dirs, all_dirs, freqs)), out_s...  4.78 us

profile of v4, /device:TPU:2, one launch (start us, length us, event | category | flops | bytes accessed | tf_op | source)
XLA Modules:
  0.0 73.5 jit_solution(15089947589924984375)
XLA Ops:
  0.0 68.7 %shard_map.82 = (f32[9,32,8,512]{3,2,1,0:T(8,128)}, f32[2,8,512]{2,1,0:T(8,128)}) custom-call(f32[148]{0:T(256)} %constant.2.clone.circle_ref, f32[9,32,8,512]{3,2,1,0:T(8,128)} %x_hbm.1, s32[8,512]{1,0:T(8,128)} %mask_ref.1, s32[8,512]{1,0:T(8,128)} %class_hbm.1, f32[2,8,512]{2,1,0:T(8,128)} %slope_hbm.1, f32[4,32]{1,0:T(4,128)} %table_hbm.1, f32[1,32]{1,0:T(1,128)} %bitcast.1), custom_call_target="tpu_custom_call" | custom-call | tf_op jit(solution)/shard_map/pallas_call | solution.py:481
  68.7 4.8 %shard_map.83 = f32[9,32,8,512]{3,2,1,0:T(8,128)} custom-call(f32[148]{0:T(256)} %constant.2.clone.circle_ref, f32[9,32,8,512]{3,2,1,0:T(8,128)} %get-tuple-element.7.q_hbm, f32[2,8,512]{2,1,0:T(8,128)} %get-tuple-element.8.sums_ref, f32[2,8,512]{2,1,0:T(8,128)} %wind_ref.1, s32[8,512]{1,0:T(8,128)} %mask_ref.1), custom_call_target="tpu_custom_call" | custom-call | tf_op jit(solution)/shard_map/pallas_call | solution.py:528
